TPU v7x, 32 devices: a whole 2x2x4 slice. The times are simulated.
32 devices in a mesh: groups: 2 (over y), ep: 4 (over z), node: 2 (over x), pair: 2 (over core).
Axes of the slice: x: 2, y: 2, z: 4, core: 2. Of those that a mesh axis runs over, the one named last changes fastest.
Arguments:
- rows_in: bfloat16 [256, 7168], P(('groups', 'ep', 'node', 'pair')), parts along dimension 0, may hold values from -6 to 6
- expert_ids: int32 [256, 2], P(('groups', 'ep', 'node', 'pair')), parts along dimension 0, may hold values from 0 to 3, all different within a row; in each aligned block of 8 rows (0 to 7, 8 to 15, ...) at most 8 rows name the same one
- gates: float32 [256, 2], P(('groups', 'ep', 'node', 'pair')), parts along dimension 0, may hold values from 0.2 to 1
- copy_expert: int32 [4], replicated, may hold values from 0 to 3, as said below
- gate_slots: bfloat16 [4, 2, 7168, 1024], P('ep', None, None, ('node', 'pair')), as said below
- up_slots: bfloat16 [4, 2, 7168, 1024], P('ep', None, None, ('node', 'pair')), as said below
- down_slots: bfloat16 [4, 2, 1024, 7168], P('ep', None, ('node', 'pair')), as said below
Outputs:
- combined: bfloat16 [256, 7168], P(('groups', 'ep', 'node', 'pair')), parts along dimension 0
There are 2 independent parts, one for each index of `groups`. A program takes and returns all parts, laid end to end along the dimension named above; an argument that names none is the same for every part. Nothing has to cross between parts.
Inputs may be any that keep to these rules, and one draw needn't show every extreme that they name: `expert_ids`: in each aligned block of 8 rows (the rows of one device) no expert is named by more than 8 rows, and some block has an expert named by exactly 8. `copy_expert`: a permutation of the 4 experts. `gate_slots`: slot 0 of group g holds expert g; slot 1 of group g holds exactly the weights of slot 0 of group copy_expert[g]. `up_slots`: as for gate_slots. `down_slots`: as for gate_slots.
All inputs are finite; a program needn't handle non-finite values.
Results may differ from a plain program's by a relative error of at most 0.0085.
Values may be sent and summed in bfloat16 or wider, within the bound.
A program may use at most 64 MiB of HBM per device.

v0:
```python
import jax
import jax.numpy as jnp
from jax import lax
from jax.sharding import PartitionSpec as P


def expert_hidden(inputs, gate_pair, up_pair):
    gate_act = jnp.einsum("nshd,sdf->nshf", inputs, gate_pair, preferred_element_type=jnp.float32)
    up_act = jnp.einsum("nshd,sdf->nshf", inputs, up_pair, preferred_element_type=jnp.float32)
    return (jax.nn.silu(gate_act) * up_act).astype(jnp.bfloat16)


def expert_share(hidden, down_pair):
    return jnp.einsum(
        "nshf,sfd->nshd", hidden, down_pair, preferred_element_type=jnp.float32
    ).astype(jnp.bfloat16)


def per_device(rows_in, expert_ids, gates, copy_expert, gate_slots, up_slots, down_slots):
    row_count, pick_count = expert_ids.shape
    group_count = copy_expert.shape[0]
    model_width = rows_in.shape[1]
    half_cap = row_count * pick_count // group_count
    buffer_rows = group_count * 2 * half_cap
    picked = expert_ids.reshape(-1)
    expert_list = jnp.arange(group_count, dtype=jnp.int32)
    named_mask = (picked[:, None] == expert_list[None, :]).astype(jnp.int32)
    earlier = jnp.cumsum(named_mask, axis=0) - named_mask
    ordinal = jnp.sum(earlier * named_mask, axis=1)
    holder = jnp.sum(
        jnp.where(copy_expert[None, :] == expert_list[:, None], expert_list[None, :], 0), axis=1
    )
    copy_group = jnp.sum(named_mask * holder[None, :], axis=1)
    parity = ordinal % 2
    target_group = jnp.where(parity == 0, picked, copy_group)
    location = (target_group * 2 + parity) * half_cap + ordinal // 2
    routing = location[:, None] == jnp.arange(buffer_rows, dtype=jnp.int32)[None, :]
    by_row = routing.reshape(row_count, pick_count, buffer_rows)
    placing = jnp.sum(by_row.astype(jnp.float32), axis=1).astype(jnp.bfloat16)
    weighting = jnp.sum(by_row.astype(jnp.float32) * gates[:, :, None], axis=1)
    outgoing = jnp.dot(placing.T, rows_in, preferred_element_type=jnp.float32).astype(jnp.bfloat16)
    outgoing = outgoing.reshape(group_count, 2, half_cap, model_width)
    gate_pair = gate_slots[0]
    up_pair = up_slots[0]
    down_pair = down_slots[0]
    sharers = lax.axis_size("node") * lax.axis_size("pair")
    copies = jnp.broadcast_to(outgoing[:, None], (group_count, sharers, 2, half_cap, model_width))
    copies = copies.reshape(group_count * sharers, 2, half_cap, model_width)
    partial_out = expert_share(
        expert_hidden(
            lax.all_to_all(copies, ("ep", "node", "pair"), split_axis=0, concat_axis=0, tiled=True),
            gate_pair,
            up_pair,
        ),
        down_pair,
    )
    answered = lax.all_to_all(
        partial_out, ("ep", "node", "pair"), split_axis=0, concat_axis=0, tiled=True
    )
    returned = jnp.sum(
        answered.reshape(group_count, sharers, 2, half_cap, model_width), axis=1, dtype=jnp.float32
    )
    combined = jnp.dot(
        weighting,
        returned.reshape(buffer_rows, model_width),
        precision=lax.Precision.HIGHEST,
        preferred_element_type=jnp.float32,
    )
    return combined.astype(jnp.bfloat16)


def solution(mesh):
    in_specs = (
        P(("groups", "ep", "node", "pair"), None),
        P(("groups", "ep", "node", "pair"), None),
        P(("groups", "ep", "node", "pair"), None),
        P(),
        P("ep", None, None, ("node", "pair")),
        P("ep", None, None, ("node", "pair")),
        P("ep", None, ("node", "pair"), None),
    )
    out_specs = P(("groups", "ep", "node", "pair"), None)
    return jax.shard_map(
        per_device, mesh=mesh, in_specs=in_specs, out_specs=out_specs, check_vma=False
    )
```

profile of v0, /device:TPU:0, one launch (start us, length us, event | category | flops | bytes accessed | tf_op | source)
XLA Modules:
  0.0 113.3 jit_solution(17780255907711462853)
XLA Ops:
  0.0 0.0 copy-start
  0.0 0.8 select_reduce_fusion.3
  0.8 0.8 copy.31
  1.6 0.1 eq.51
  1.6 0.1 fusion.28
  1.8 0.2 select_reduce_fusion.2
  1.9 0.1 reduce_sum.59
  2.0 0.1 reduce_sum.62
  2.1 0.1 copy.33
  2.2 0.8 convert_reduce_fusion.1
  3.0 0.3 convolution_convert_fusion.1
  3.3 0.2 broadcast_in_dim.18
  3.5 0.7 broadcast_in_dim.30
  4.2 0.0 slice-start
  4.2 0.0 slice-start.2
  4.2 50.2 %all_to_all.10 = bf16[16,2,4,7168]{3,2,1,0:T(4,128)(2,1)S(1)} all-to-all(bf16[16,2,4,7168]{3,2,1,0:T(4,128)(2,1)S(1)} %bitcast.47), channel_id=1, replica_groups=mesh['groups'=2,'ep'=4,'node'=2,'pair'=2] {'ep','node','pair'}, dimensions={0} | all-to-all | bytes 3670016 | tf_op jit(solution)/shard_map/all_to_all | solution.py:51
  54.4 5.1 %fusion.8 = f32[16,2,4,256]{3,0,2,1:T(8,128)S(1)} fusion(bf16[1,2,7168,256]{3,2,1,0:T(8,128)(2,1)} %param.11, bf16[16,2,4,7168]{3,2,1,0:T(4,128)(2,1)S(1)} %all_to_all.10), kind=kOutput, calls=%fused_computation.12 | convolution fusion | flops 469762048 | bytes 9306112 | tf_op jit(solution)/shard_map/nshd,sdf->nshf/dot_general | solution.py:8
  59.6 1.8 %fusion.23 = bf16[16,2,4,256]{3,0,2,1:T(8,128)(2,1)S(1)} fusion(bf16[1,2,7168,256]{3,2,1,0:T(8,128)(2,1)S(1)} %bitcast.46, bf16[16,2,4,7168]{3,2,1,0:T(4,128)(2,1)S(1)} %all_to_all.10, f32[16,2,4,256]{3,0,2,1:T(8,128)S(1)} %fusion.8), kind=kOutput, calls=%fused_computation.15 | convolution fusion | flops 469958656 | bytes 9371648 | tf_op jit(solution)/shard_map/nshd,sdf->nshf/dot_general | solution.py:9
  61.4 1.4 %fusion = bf16[16,2,4,7168]{3,0,2,1:T(8,128)(2,1)S(1)} fusion(bf16[16,2,4,256]{3,0,2,1:T(8,128)(2,1)S(1)} %fusion.23, bf16[1,2,256,7168]{3,2,1,0:T(8,128)(2,1)S(1)} %bitcast.49), kind=kOutput, calls=%fused_computation.1 | convolution fusion | flops 470679552 | bytes 9240576 | tf_op jit(solution)/shard_map/nshf,sfd->nshd/dot_general | solution.py:14
  62.8 1.4 %copy.36 = bf16[16,2,4,7168]{3,2,1,0:T(4,128)(2,1)S(1)} copy(bf16[16,2,4,7168]{3,0,2,1:T(8,128)(2,1)S(1)} %fusion) | data formatting | bytes 3670016 | tf_op jit(solution)/shard_map/convert_element_type | solution.py:16
  64.3 46.6 %all_to_all.11 = bf16[16,2,4,7168]{3,2,1,0:T(4,128)(2,1)S(1)} all-to-all(bf16[16,2,4,7168]{3,2,1,0:T(4,128)(2,1)S(1)} %copy.36), channel_id=1, replica_groups=mesh['groups'=2,'ep'=4,'node'=2,'pair'=2] {'ep','node','pair'}, dimensions={0} | all-to-all | bytes 3670016 | tf_op jit(solution)/shard_map/all_to_all | solution.py:57
  110.8 0.9 convert_reduce_fusion
  111.8 0.3 reshape.66
  112.1 1.2 %convolution_convert_fusion.2 = bf16[8,7168]{1,0:T(8,128)(2,1)} fusion(f32[8,32]{1,0:T(8,128)S(1)} %get-tuple-element.6, f32[32,7168]{1,0:T(8,128)S(1)} %reshape.66), kind=kOutput, calls=%fused_computation.3 | convolution fusion | flops 22077440 | bytes 1033216 | tf_op jit(solution)/shard_map/dot_general | solution.py:63
  (11 shorter events, 0.1 us)
Async XLA Ops:
  0.0 3.0 %copy-start = (bf16[8,7168]{1,0:T(8,128)(2,1)S(1)}, bf16[8,7168]{1,0:T(8,128)(2,1)}, u32[]{:S(2)}) copy-start(bf16[8,7168]{1,0:T(8,128)(2,1)} %param.7) | copy-start | bytes 344068
  4.2 55.4 %slice-start = ((s8[7340032]{0:T(1024)(128)(4,1)}), s8[4194304]{0:T(1024)(128)(4,1)S(1)}, s32[]{:S(2)}) async-start(s8[7340032]{0:T(1024)(128)(4,1)} %bitcast.45), calls=%async_computation.2 | async-start | bytes 8388608
  4.2 57.2 %slice-start.2 = ((s8[7340032]{0:T(1024)(128)(4,1)}), s8[4194304]{0:T(1024)(128)(4,1)S(1)}, s32[]{:S(2)}) async-start(s8[7340032]{0:T(1024)(128)(4,1)} %bitcast.48), calls=%async_computation.4 | async-start | bytes 8388608
  54.4 5.2 %slice-start.1 = ((s8[7340032]{0:T(1024)(128)(4,1)}), s8[3145728]{0:T(1024)(128)(4,1)S(1)}, s32[]{:S(2)}) async-start(s8[7340032]{0:T(1024)(128)(4,1)} %bitcast.45), calls=%async_computation.3 | async-start | bytes 6291456
  54.4 7.0 %slice-start.3 = ((s8[7340032]{0:T(1024)(128)(4,1)}), s8[3145728]{0:T(1024)(128)(4,1)S(1)}, s32[]{:S(2)}) async-start(s8[7340032]{0:T(1024)(128)(4,1)} %bitcast.48), calls=%async_computation.5 | async-start | bytes 6291456
where the time goes:
time: 114 us; the launch traced here: 113 us
  blocking collectives  96.7 us (85%)
  matrix products  9.88 us (9%)
  local copies, waits for them, and re-layouts  3.71 us (3%)
  other arithmetic  2.82 us (2%)
    all_to_all x1, blocking collectives, per_device(): lax.all_to_all(copies, ('ep', 'node', 'pair'), split_axis=0, concat_axis=...  50.2 us
    all_to_all x1, blocking collectives, per_device(): lax.all_to_all(partial_out, ('ep', 'node', 'pair'), split_axis=0, concat_...  46.6 us
    dot_general x1, matrix products, expert_hidden(): jnp.einsum('nshd,sdf->nshf', inputs, gate_pair, preferred_element_type=jn...  5.14 us

commit v1 on v0

v1 whole, which is shorter than its diff:
```python
import functools

import jax
import jax.numpy as jnp
from jax import lax
from jax.experimental import pallas as pl
from jax.experimental.pallas import tpu as pltpu
from jax.sharding import PartitionSpec as P

COLUMN_BLOCKS = 4
ROW_BLOCKS_PER_DOT = 16


def flip(a, b, size):
    if size & (size - 1):
        return lax.rem(a + b, size)
    out, bit = 0, 1
    while bit < size:
        p, q = (a // bit) % 2, (b // bit) % 2
        out = out + bit * (p + q - 2 * p * q)
        bit *= 2
    return out


def kernel(
    sizes,
    rows_ref, ids_ref, gates_ref, gate_hbm, up_hbm, down_hbm,
    out_ref,
    w_gate, w_up, w_down, rows, acc_gate, acc_up, hidden, part, part_in, node_in, sums, answers,
    w_sem, own_sem, zs, zr, xs, xr, ps, pr, ps2, pr2, xs2, xr2, zs2, zr2,
):
    n_ep, n_node, n_pair, steps = sizes
    z, x, c = lax.axis_index("ep"), lax.axis_index("node"), lax.axis_index("pair")
    blocks = rows.shape[1]
    height, cols = rows.shape[2], rows.shape[3]
    half = n_node * n_ep
    other = 1 - c
    z_order = [flip(z, s, n_ep) for s in range(n_ep)]
    x_others = [lax.rem(x + d, n_node) for d in range(1, n_node)]

    def block_of(cc, xx, zz):
        return (cc * n_node + xx) * n_ep + zz

    def remote(src, dst, send, recv, **to):
        return pltpu.make_async_remote_copy(
            src_ref=src, dst_ref=dst, send_sem=send, recv_sem=recv,
            device_id=to, device_id_type=pl.DeviceIdType.MESH,
        )

    def cut(j):
        return pl.ds(j * cols, cols)

    local = []
    for j in range(steps):
        local.append([
            pltpu.make_async_copy(gate_hbm.at[0, 0, cut(j), :], w_gate.at[j], w_sem.at[0, j]),
            pltpu.make_async_copy(up_hbm.at[0, 0, cut(j), :], w_up.at[j], w_sem.at[1, j]),
            pltpu.make_async_copy(down_hbm.at[0, 0, :, cut(j)], w_down.at[j], w_sem.at[2, j]),
            pltpu.make_async_copy(rows_ref.at[:, cut(j)], rows.at[j, block_of(c, x, z)], own_sem.at[j]),
        ])
    for j in range(steps):
        local[j][3].start()

    barrier = pltpu.get_barrier_semaphore()
    peers = [dict(ep=zz) for zz in z_order[1:]] + [dict(node=xx) for xx in x_others] + [dict(pair=other)]
    for to in peers:
        pl.semaphore_signal(barrier, inc=1, device_id=to, device_id_type=pl.DeviceIdType.MESH)
    for j in range(steps):
        for copy in local[j][:3]:
            copy.start()
    pl.semaphore_wait(barrier, len(peers))

    sends = []

    def go(copy):
        copy.start()
        sends.append(copy)

    def own_out(j):
        mine = rows_ref.at[:, cut(j)]
        slot = rows.at[j, block_of(c, x, z)]
        for zz in reversed(z_order[1:]):
            go(remote(mine, slot, zs.at[j, zz], zr.at[j, z], ep=zz))
        for xx in x_others:
            go(remote(mine, slot, xs.at[j, z, xx], xr.at[j, z, x], node=xx))

    def forward_nodes(j):
        for zz in z_order[1:]:
            slot = rows.at[j, block_of(c, x, zz)]
            remote(slot, slot, zs.at[j, zz], zr.at[j, zz], ep=zz).wait_recv()
            for xx in x_others:
                go(remote(slot, slot, xs.at[j, zz, xx], xr.at[j, zz, x], node=xx))

    def forward_pair(j):
        for zz in z_order:
            for xx in x_others:
                slot = rows.at[j, block_of(c, xx, zz)]
                remote(slot, slot, xs.at[j, zz, xx], xr.at[j, zz, xx], node=xx).wait_recv()
        local[j][3].wait()
        mine = rows.at[j, pl.ds(c * half, half)]
        go(remote(mine, mine, ps.at[j], pr.at[j], pair=other))

    group = min(ROW_BLOCKS_PER_DOT, blocks)

    def tiles(body):
        if blocks == group:
            body(0)
        else:
            lax.fori_loop(0, blocks // group, lambda i, _: (body(i), 0)[1], 0)

    def into(j):
        theirs = rows.at[j, pl.ds(other * half, half)]
        remote(theirs, theirs, ps.at[j], pr.at[j], pair=other).wait_recv()
        local[j][0].wait()
        local[j][1].wait()

        def body(i):
            data = rows[j, pl.ds(i * group, group)].astype(jnp.float32)
            data = data.reshape(group * height, cols).astype(jnp.bfloat16)
            for acc, weight in ((acc_gate, w_gate), (acc_up, w_up)):
                value = jnp.dot(data, weight[j], preferred_element_type=jnp.float32)
                if j == 0:
                    acc[i] = value
                else:
                    acc[i] += value
        tiles(body)

    def activate():
        def body(i):
            gate = acc_gate[i]
            hidden[i] = (gate / (1.0 + jnp.exp(-gate)) * acc_up[i]).astype(jnp.bfloat16)
        tiles(body)

    def down(j):
        local[j][2].wait()

        def body(i):
            value = jnp.dot(hidden[i], w_down[j], preferred_element_type=jnp.float32)
            part[j, pl.ds(i * group, group)] = value.reshape(group, height, cols).astype(jnp.bfloat16)
        tiles(body)
        go(remote(part.at[j, pl.ds(other * half, half)], part_in.at[j], ps2.at[j], pr2.at[j], pair=other))

    def sum_pair(j):
        remote(part_in.at[j], part_in.at[j], ps2.at[j], pr2.at[j], pair=other).wait_recv()
        for xx in x_others + [x]:
            here = pl.ds(xx * n_ep, n_ep)
            mine = part[j, pl.ds(c * half + xx * n_ep, n_ep)].astype(jnp.float32)
            part_in[j, here] = (part_in[j, here].astype(jnp.float32) + mine).astype(jnp.bfloat16)
        for xx in x_others:
            go(remote(part_in.at[j, pl.ds(xx * n_ep, n_ep)], node_in.at[j, x],
                      xs2.at[j, xx], xr2.at[j, x], node=xx))

    def sum_nodes(j):
        total = part_in[j, pl.ds(x * n_ep, n_ep)].astype(jnp.float32)
        for xx in x_others:
            slot = node_in.at[j, xx]
            remote(slot, slot, xs2.at[j, xx], xr2.at[j, xx], node=xx).wait_recv()
            total = total + node_in[j, xx].astype(jnp.float32)
        sums[j] = total.astype(jnp.bfloat16)
        for zz in reversed(z_order[1:]):
            go(remote(sums.at[j, zz], answers.at[j, z], zs2.at[j, zz], zr2.at[j, z], ep=zz))

    def weight_of(zz):
        return jnp.sum(jnp.where(ids_ref[...] == zz, gates_ref[...], 0.0), axis=1, keepdims=True)

    def finish(j):
        total = None
        for zz in z_order:
            if zz is z_order[0]:
                value = sums[j, zz].astype(jnp.float32)
            else:
                slot = answers.at[j, zz]
                remote(slot, slot, zs2.at[j, zz], zr2.at[j, zz], ep=zz).wait_recv()
                value = answers[j, zz].astype(jnp.float32)
            share = weight_of(zz)
            value = jnp.where(share > 0.0, share * value, 0.0)
            total = value if total is None else total + value
        out_ref[:, cut(j)] = total.astype(jnp.bfloat16)

    for j in range(steps):
        own_out(j)
    for t in range(steps + 2):
        if t < steps:
            forward_nodes(t)
        if 0 <= t - 1 < steps:
            forward_pair(t - 1)
        if 0 <= t - 2 < steps:
            into(t - 2)
    activate()
    for t in range(steps + 1):
        if t < steps:
            down(t)
        if t >= 1:
            sum_pair(t - 1)
    for j in range(steps):
        sum_nodes(j)
    for j in range(steps):
        finish(j)
    for copy in sends:
        copy.wait_send()


def solution(mesh):
    n_ep, n_node, n_pair = (mesh.shape[name] for name in ("ep", "node", "pair"))
    steps = COLUMN_BLOCKS

    def per_device(rows_in, expert_ids, gates, copy_expert, gate_slots, up_slots, down_slots):
        height, width = rows_in.shape
        units = gate_slots.shape[3]
        cols = width // steps
        blocks = n_ep * n_node * n_pair
        group = min(ROW_BLOCKS_PER_DOT, blocks)
        bf16, f32 = jnp.bfloat16, jnp.float32
        dma = pltpu.SemaphoreType.DMA
        anywhere = pl.BlockSpec(memory_space=pl.ANY)
        vmem = pl.BlockSpec(memory_space=pltpu.VMEM)
        return pl.pallas_call(
            functools.partial(kernel, (n_ep, n_node, n_pair, steps)),
            out_shape=jax.ShapeDtypeStruct((height, width), bf16),
            in_specs=[anywhere, vmem, vmem, anywhere, anywhere, anywhere],
            out_specs=vmem,
            scratch_shapes=[
                pltpu.VMEM((steps, cols, units), bf16),
                pltpu.VMEM((steps, cols, units), bf16),
                pltpu.VMEM((steps, units, cols), bf16),
                pltpu.VMEM((steps, blocks, height, cols), bf16),
                pltpu.VMEM((blocks // group, group * height, units), f32),
                pltpu.VMEM((blocks // group, group * height, units), f32),
                pltpu.VMEM((blocks // group, group * height, units), bf16),
                pltpu.VMEM((steps, blocks, height, cols), bf16),
                pltpu.VMEM((steps, n_ep * n_node, height, cols), bf16),
                pltpu.VMEM((steps, n_node, n_ep, height, cols), bf16),
                pltpu.VMEM((steps, n_ep, height, cols), bf16),
                pltpu.VMEM((steps, n_ep, height, cols), bf16),
                dma((3, steps)), dma((steps,)),
                dma((steps, n_ep)), dma((steps, n_ep)),
                dma((steps, n_ep, n_node)), dma((steps, n_ep, n_node)),
                dma((steps,)), dma((steps,)),
                dma((steps,)), dma((steps,)),
                dma((steps, n_node)), dma((steps, n_node)),
                dma((steps, n_ep)), dma((steps, n_ep)),
            ],
            compiler_params=pltpu.CompilerParams(
                collective_id=0, has_side_effects=True, vmem_limit_bytes=60 * 1024 * 1024
            ),
        )(rows_in, expert_ids, gates, gate_slots, up_slots, down_slots)

    spec = P(("groups", "ep", "node", "pair"), None)
    return jax.shard_map(
        per_device,
        mesh=mesh,
        in_specs=(
            spec, spec, spec, P(),
            P("ep", None, None, ("node", "pair")),
            P("ep", None, None, ("node", "pair")),
            P("ep", None, ("node", "pair"), None),
        ),
        out_specs=spec,
        check_vma=False,
    )
```

time: 114 us -> 48.1 us (0.42)
  blocking collectives: 96.7 us -> 0 us
  Pallas kernels: 0 us -> 43.6 us
  matrix products: 9.88 us -> 0 us
  other arithmetic: 2.82 us -> 0 us
    all_to_all x2 -> x0, blocking collectives: 96.7 us -> none  [the longest x1 50.2 us: per_device(): lax.all_to_all(copies, ('ep', 'node', 'pair'), split_axis=0, concat_axis=...]
    pallas_call x0 -> x1, Pallas kernels: none -> 43.6 us  [per_device(): pl.pallas_call(functools.partial(kernel, (n_ep, n_node, n_pair, steps)),...]
    dot_general x5 -> x0, matrix products: 9.88 us -> none  [the longest x1 5.14 us: expert_hidden(): jnp.einsum('nshd,sdf->nshf', inputs, gate_pair, preferred_element_type=jn...]
    unnamed x11 -> x3, local copies, waits for them, and re-layouts: 0.78 us -> 4.24 us
    reduce_sum x4 -> x0, other arithmetic: 2.69 us -> none  [the longest x1 0.93 us: per_device(): jnp.sum(answered.reshape(group_count, sharers, 2, half_cap, model_width),...]
    convert_element_type x1 -> x0, local copies, waits for them, and re-layouts: 1.42 us -> none  [expert_share(): return jnp.einsum('nshf,sfd->nshd', hidden, down_pair, preferred_element_...]
where the time goes in v1:
time: 48.1 us; the launch traced here: 47.9 us
  Pallas kernels  43.6 us (91%)
  local copies, waits for them, and re-layouts  4.24 us (9%)
    pallas_call x1, Pallas kernels, per_device(): pl.pallas_call(functools.partial(kernel, (n_ep, n_node, n_pair, steps)),...  43.6 us
    unnamed x3, local copies, waits for them, and re-layouts  4.24 us

profile of v1, /device:TPU:0, one launch (start us, length us, event | category | flops | bytes accessed | tf_op | source)
XLA Modules:
  0.0 47.9 jit_solution(11608535083496202788)
XLA Ops:
  0.0 1.3 %copy.7.ids_ref = s32[8,2]{1,0:T(8,128)} copy(s32[8,2]{0,1:T(2,128)} %param.8) | data formatting | bytes 128 | tf_op args[1]
  1.3 1.3 %copy.8.gates_ref = f32[8,2]{1,0:T(8,128)} copy(f32[8,2]{0,1:T(2,128)} %param.9) | data formatting | bytes 128 | tf_op args[2]
  2.7 43.6 %shard_map.64 = bf16[8,7168]{1,0:T(8,128)(2,1)} custom-call(bf16[8,7168]{1,0:T(8,128)(2,1)} %rows_ref.1, s32[8,2]{1,0:T(8,128)} %copy.7.ids_ref, f32[8,2]{1,0:T(8,128)} %copy.8.gates_ref, bf16[1,2,7168,256]{3,2,1,0:T(8,128)(2,1)} %gate_hbm.1, bf16[1,2,7168,256]{3,2,1,0:T(8,128)(2,1)} %up_hbm.1, bf16[1,2,256,7168]{3,2,1,0:T(8,128)(2,1)} %down_hbm.1), custom_call_target="tpu_custom_call" | custom-call | tf_op jit(solution)/shard_map/pallas_call | solution.py:217
  46.3 1.6 %copy.10 = bf16[8,7168]{1,0:T(8,128)(2,1)} copy(bf16[8,7168]{1,0:T(8,128)(2,1)} %shard_map.64) | data formatting | bytes 229376

commit v2 on v1

--- a/solution.py
+++ b/solution.py
@@ -8,6 +8,7 @@
 from jax.sharding import PartitionSpec as P
 
 COLUMN_BLOCKS = 4
+AHEAD = 2
 ROW_BLOCKS_PER_DOT = 16
 
 
@@ -79,7 +80,7 @@
     def own_out(j):
         mine = rows_ref.at[:, cut(j)]
         slot = rows.at[j, block_of(c, x, z)]
-        for zz in reversed(z_order[1:]):
+        for zz in z_order[1:]:
             go(remote(mine, slot, zs.at[j, zz], zr.at[j, z], ep=zz))
         for xx in x_others:
             go(remote(mine, slot, xs.at[j, z, xx], xr.at[j, z, x], node=xx))
@@ -146,6 +147,8 @@
             here = pl.ds(xx * n_ep, n_ep)
             mine = part[j, pl.ds(c * half + xx * n_ep, n_ep)].astype(jnp.float32)
             part_in[j, here] = (part_in[j, here].astype(jnp.float32) + mine).astype(jnp.bfloat16)
+
+    def send_nodes(j):
         for xx in x_others:
             go(remote(part_in.at[j, pl.ds(xx * n_ep, n_ep)], node_in.at[j, x],
                       xs2.at[j, xx], xr2.at[j, x], node=xx))
@@ -157,11 +160,14 @@
             remote(slot, slot, xs2.at[j, xx], xr2.at[j, xx], node=xx).wait_recv()
             total = total + node_in[j, xx].astype(jnp.float32)
         sums[j] = total.astype(jnp.bfloat16)
-        for zz in reversed(z_order[1:]):
+        for zz in z_order[1:]:
             go(remote(sums.at[j, zz], answers.at[j, z], zs2.at[j, zz], zr2.at[j, z], ep=zz))
 
     def weight_of(zz):
-        return jnp.sum(jnp.where(ids_ref[...] == zz, gates_ref[...], 0.0), axis=1, keepdims=True)
+        named = jnp.sum(jnp.where(ids_ref[...] == zz, gates_ref[...], 0.0), axis=0, keepdims=True)
+        square = (height, height)
+        diagonal = lax.broadcasted_iota(jnp.int32, square, 0) == lax.broadcasted_iota(jnp.int32, square, 1)
+        return jnp.sum(jnp.where(diagonal, jnp.broadcast_to(named, square), 0.0), axis=1, keepdims=True)
 
     def finish(j):
         total = None
@@ -177,11 +183,14 @@
             total = value if total is None else total + value
         out_ref[:, cut(j)] = total.astype(jnp.bfloat16)
 
-    for j in range(steps):
+    ahead = min(AHEAD, steps)
+    for j in range(ahead):
         own_out(j)
     for t in range(steps + 2):
         if t < steps:
             forward_nodes(t)
+        if t + ahead < steps:
+            own_out(t + ahead)
         if 0 <= t - 1 < steps:
             forward_pair(t - 1)
         if 0 <= t - 2 < steps:
@@ -192,10 +201,15 @@
             down(t)
         if t >= 1:
             sum_pair(t - 1)
-    for j in range(steps):
-        sum_nodes(j)
-    for j in range(steps):
-        finish(j)
+            if t - 1 < ahead:
+                send_nodes(t - 1)
+    for t in range(steps + 2):
+        if t < steps:
+            sum_nodes(t)
+        if t + ahead < steps:
+            send_nodes(t + ahead)
+        if t >= 2:
+            finish(t - 2)
     for copy in sends:
         copy.wait_send()
 
@@ -243,7 +257,7 @@
             compiler_params=pltpu.CompilerParams(
                 collective_id=0, has_side_effects=True, vmem_limit_bytes=60 * 1024 * 1024
             ),
-        )(rows_in, expert_ids, gates, gate_slots, up_slots, down_slots)
+        )(rows_in, expert_ids.T, gates.T, gate_slots, up_slots, down_slots)
 
     spec = P(("groups", "ep", "node", "pair"), None)
     return jax.shard_map(

time: 48.1 us -> 43.8 us (0.911)
  local copies, waits for them, and re-layouts: 4.24 us -> 1.55 us
  Pallas kernels: 43.6 us -> 42 us
    unnamed x3 -> x1, local copies, waits for them, and re-layouts: 4.24 us -> 1.55 us
    pallas_call x1, Pallas kernels: 43.6 us -> 42 us  [per_device(): pl.pallas_call(functools.partial(kernel, (n_ep, n_node, n_pair, steps)),...]
where the time goes in v2:
time: 43.8 us; the launch traced here: 43.6 us
  Pallas kernels  42 us (96%)
  local copies, waits for them, and re-layouts  1.55 us (4%)
    pallas_call x1, Pallas kernels, per_device(): pl.pallas_call(functools.partial(kernel, (n_ep, n_node, n_pair, steps)),...  42 us
    unnamed x1, local copies, waits for them, and re-layouts  1.55 us

profile of v2, /device:TPU:0, one launch (start us, length us, event | category | flops | bytes accessed | tf_op | source)
XLA Modules:
  0.0 43.6 jit_solution(860407645652847917)
XLA Ops:
  0.0 42.0 %shard_map.64 = bf16[8,7168]{1,0:T(8,128)(2,1)} custom-call(bf16[8,7168]{1,0:T(8,128)(2,1)} %rows_ref.1, s32[2,8]{1,0:T(2,128)} %bitcast.2, f32[2,8]{1,0:T(2,128)} %bitcast.3, bf16[1,2,7168,256]{3,2,1,0:T(8,128)(2,1)} %gate_hbm.1, bf16[1,2,7168,256]{3,2,1,0:T(8,128)(2,1)} %up_hbm.1, bf16[1,2,256,7168]{3,2,1,0:T(8,128)(2,1)} %down_hbm.1), custom_call_target="tpu_custom_call" | custom-call | tf_op jit(solution)/shard_map/pallas_call | solution.py:231
  42.1 1.6 %copy.8 = bf16[8,7168]{1,0:T(8,128)(2,1)} copy(bf16[8,7168]{1,0:T(8,128)(2,1)} %shard_map.64) | data formatting | bytes 229376

commit v3 on v2

v3 whole, which is shorter than its diff:
```python
import functools

import jax
import jax.numpy as jnp
from jax import lax
from jax.experimental import pallas as pl
from jax.experimental.pallas import tpu as pltpu
from jax.sharding import PartitionSpec as P

GATHER_SPLIT = (14, 14, 14, 14)
RETURN_SPLIT = (14, 14, 14, 14)
GATHER_AHEAD = 2
RETURN_AHEAD = 2
ROW_BLOCKS_PER_DOT = 16


def flip(a, b, size):
    if size & (size - 1):
        return lax.rem(a + b, size)
    out, bit = 0, 1
    while bit < size:
        p, q = (a // bit) % 2, (b // bit) % 2
        out = out + bit * (p + q - 2 * p * q)
        bit *= 2
    return out


def kernel(
    sizes,
    rows_ref, ids_hbm, gates_hbm, gate_hbm, up_hbm, down_hbm,
    out_hbm,
    ids_ref, gates_ref, out_ref, w_gate, w_up, w_down, rows, acc_gate, acc_up, hidden, part, part_in, node_in, sums, answers,
    w_sem, own_sem, out_sem, zs, zr, xs, xr, ps, pr, ps2, pr2, xs2, xr2, zs2, zr2,
):
    n_ep, n_node, n_pair = sizes
    z, x, c = lax.axis_index("ep"), lax.axis_index("node"), lax.axis_index("pair")
    blocks, height = rows.shape[0], rows.shape[1]
    half = n_node * n_ep
    other = 1 - c
    z_order = [flip(z, s, n_ep) for s in range(n_ep)]
    x_others = [lax.rem(x + d, n_node) for d in range(1, n_node)]

    def block_of(cc, xx, zz):
        return (cc * n_node + xx) * n_ep + zz

    def remote(src, dst, send, recv, **to):
        return pltpu.make_async_remote_copy(
            src_ref=src, dst_ref=dst, send_sem=send, recv_sem=recv,
            device_id=to, device_id_type=pl.DeviceIdType.MESH,
        )

    def cut_in(j):
        return pl.ds(sum(GATHER_SPLIT[:j]) * 128, GATHER_SPLIT[j] * 128)

    def cut_out(j):
        return pl.ds(sum(RETURN_SPLIT[:j]) * 128, RETURN_SPLIT[j] * 128)

    steps, steps_out = len(GATHER_SPLIT), len(RETURN_SPLIT)

    own = rows.at[block_of(c, x, z)]
    own_copy = pltpu.make_async_copy(rows_ref, own, own_sem.at[0])
    own_copy.start()
    ids_copy = pltpu.make_async_copy(ids_hbm, ids_ref, own_sem.at[1])
    gates_copy = pltpu.make_async_copy(gates_hbm, gates_ref, own_sem.at[2])
    outs = [
        pltpu.make_async_copy(out_ref.at[:, cut_out(j)], out_hbm.at[:, cut_out(j)], out_sem.at[j])
        for j in range(steps_out)
    ]
    weights_in = [
        [pltpu.make_async_copy(gate_hbm.at[0, 0, cut_in(j), :], w_gate.at[cut_in(j), :], w_sem.at[0, j]),
         pltpu.make_async_copy(up_hbm.at[0, 0, cut_in(j), :], w_up.at[cut_in(j), :], w_sem.at[1, j])]
        for j in range(steps)
    ]
    weights_out = [
        pltpu.make_async_copy(down_hbm.at[0, 0, :, cut_out(j)], w_down.at[:, cut_out(j)], w_sem.at[2, j])
        for j in range(steps_out)
    ]

    barrier = pltpu.get_barrier_semaphore()
    peers = [dict(ep=zz) for zz in z_order[1:]] + [dict(node=xx) for xx in x_others] + [dict(pair=other)]
    for to in peers:
        pl.semaphore_signal(barrier, inc=1, device_id=to, device_id_type=pl.DeviceIdType.MESH)
    for copy in sum(weights_in, []) + weights_out:
        copy.start()
    ids_copy.start()
    gates_copy.start()
    pl.semaphore_wait(barrier, len(peers))

    sends = []

    def go(copy):
        copy.start()
        sends.append(copy)

    def own_out(j):
        slot = rows.at[block_of(c, x, z), :, cut_in(j)]
        for zz in z_order[1:]:
            go(remote(slot, slot, zs.at[j, zz], zr.at[j, z], ep=zz))

    def own_nodes():
        slot = own
        for xx in x_others:
            go(remote(slot, slot, xs.at[0, z, xx], xr.at[0, z, x], node=xx))

    def forward_nodes(j):
        for zz in z_order[1:]:
            slot = rows.at[block_of(c, x, zz), :, cut_in(j)]
            remote(slot, slot, zs.at[j, zz], zr.at[j, zz], ep=zz).wait_recv()
            for xx in x_others:
                go(remote(slot, slot, xs.at[j, zz, xx], xr.at[j, zz, x], node=xx))

    def forward_pair(j):
        for zz in z_order[1:] if j else z_order:
            for xx in x_others:
                slot = rows.at[block_of(c, xx, zz), :, cut_in(j) if zz is not z_order[0] else slice(None)]
                remote(slot, slot, xs.at[j, zz, xx], xr.at[j, zz, xx], node=xx).wait_recv()
        mine = rows.at[pl.ds(c * half, half), :, cut_in(j)]
        go(remote(mine, mine, ps.at[j], pr.at[j], pair=other))

    group = min(ROW_BLOCKS_PER_DOT, blocks)

    def tiles(body):
        if blocks == group:
            body(0)
        else:
            lax.fori_loop(0, blocks // group, lambda i, _: (body(i), 0)[1], 0)

    def into(j):
        theirs = rows.at[pl.ds(other * half, half), :, cut_in(j)]
        remote(theirs, theirs, ps.at[j], pr.at[j], pair=other).wait_recv()
        for copy in weights_in[j]:
            copy.wait()

        def body(i):
            data = rows[pl.ds(i * group, group), :, cut_in(j)].astype(jnp.float32)
            data = data.reshape(group * height, GATHER_SPLIT[j] * 128).astype(jnp.bfloat16)
            for acc, weight in ((acc_gate, w_gate), (acc_up, w_up)):
                value = jnp.dot(data, weight[cut_in(j), :], preferred_element_type=jnp.float32)
                if j == 0:
                    acc[i] = value
                else:
                    acc[i] += value
        tiles(body)

    def activate():
        def body(i):
            gate = acc_gate[i]
            hidden[i] = (gate / (1.0 + jnp.exp(-gate)) * acc_up[i]).astype(jnp.bfloat16)
        tiles(body)

    def down(j):
        weights_out[j].wait()

        def body(i):
            value = jnp.dot(hidden[i], w_down[:, cut_out(j)], preferred_element_type=jnp.float32)
            part[pl.ds(i * group, group), :, cut_out(j)] = value.reshape(group, height, RETURN_SPLIT[j] * 128).astype(jnp.bfloat16)
        tiles(body)
        go(remote(part.at[pl.ds(other * half, half), :, cut_out(j)], part_in.at[:, :, cut_out(j)], ps2.at[j], pr2.at[j], pair=other))

    def sum_pair(j):
        remote(part_in.at[:, :, cut_out(j)], part_in.at[:, :, cut_out(j)], ps2.at[j], pr2.at[j], pair=other).wait_recv()
        for xx in x_others:
            here = pl.ds(xx * n_ep, n_ep)
            mine = part[pl.ds(c * half + xx * n_ep, n_ep), :, cut_out(j)].astype(jnp.float32)
            part_in[here, :, cut_out(j)] = (part_in[here, :, cut_out(j)].astype(jnp.float32) + mine).astype(jnp.bfloat16)

    def send_nodes(j):
        for xx in x_others:
            go(remote(part_in.at[pl.ds(xx * n_ep, n_ep), :, cut_out(j)], node_in.at[x, :, :, cut_out(j)],
                      xs2.at[j, xx], xr2.at[j, x], node=xx))

    def sum_nodes(j):
        total = part_in[pl.ds(x * n_ep, n_ep), :, cut_out(j)].astype(jnp.float32)
        total = total + part[pl.ds(c * half + x * n_ep, n_ep), :, cut_out(j)].astype(jnp.float32)
        for xx in x_others:
            slot = node_in.at[xx, :, :, cut_out(j)]
            remote(slot, slot, xs2.at[j, xx], xr2.at[j, xx], node=xx).wait_recv()
            total = total + node_in[xx, :, :, cut_out(j)].astype(jnp.float32)
        sums[:, :, cut_out(j)] = total.astype(jnp.bfloat16)
        for zz in z_order[1:]:
            go(remote(sums.at[zz, :, cut_out(j)], answers.at[z, :, cut_out(j)], zs2.at[j, zz], zr2.at[j, z], ep=zz))

    def weight_of(zz):
        named = jnp.sum(jnp.where(ids_ref[...] == zz, gates_ref[...], 0.0), axis=0, keepdims=True)
        square = (height, height)
        diagonal = lax.broadcasted_iota(jnp.int32, square, 0) == lax.broadcasted_iota(jnp.int32, square, 1)
        return jnp.sum(jnp.where(diagonal, jnp.broadcast_to(named, square), 0.0), axis=1, keepdims=True)

    def finish(j):
        total = None
        for zz in z_order:
            if zz is z_order[0]:
                value = sums[zz, :, cut_out(j)].astype(jnp.float32)
            else:
                slot = answers.at[zz, :, cut_out(j)]
                remote(slot, slot, zs2.at[j, zz], zr2.at[j, zz], ep=zz).wait_recv()
                value = answers[zz, :, cut_out(j)].astype(jnp.float32)
            share = weight_of(zz)
            value = jnp.where(share > 0.0, share * value, 0.0)
            total = value if total is None else total + value
        out_ref[:, cut_out(j)] = total.astype(jnp.bfloat16)
        outs[j].start()

    def drain():
        while sends:
            sends.pop(0).wait_send()

    own_copy.wait()
    ahead = min(GATHER_AHEAD, steps)
    for j in range(ahead):
        own_out(j)
        if j == 0:
            own_nodes()
    ahead_back = min(RETURN_AHEAD, steps_out)
    for t in range(steps + 2):
        if t < steps:
            forward_nodes(t)
        if t + ahead < steps:
            own_out(t + ahead)
        if 0 <= t - 1 < steps:
            forward_pair(t - 1)
        if 0 <= t - 2 < steps:
            into(t - 2)
    activate()
    ids_copy.wait()
    gates_copy.wait()
    for t in range(steps_out + 1):
        if t < steps_out:
            down(t)
        if t >= 1:
            sum_pair(t - 1)
            if t - 1 < ahead_back:
                send_nodes(t - 1)
    drain()
    for t in range(steps_out + 2):
        if t < steps_out:
            sum_nodes(t)
        if t + ahead_back < steps_out:
            send_nodes(t + ahead_back)
        if t >= 2:
            finish(t - 2)
    drain()
    for copy in outs:
        copy.wait()


def solution(mesh):
    n_ep, n_node, n_pair = (mesh.shape[name] for name in ("ep", "node", "pair"))
    steps = max(len(GATHER_SPLIT), len(RETURN_SPLIT))

    def per_device(rows_in, expert_ids, gates, copy_expert, gate_slots, up_slots, down_slots):
        height, width = rows_in.shape
        units = gate_slots.shape[3]
        blocks = n_ep * n_node * n_pair
        group = min(ROW_BLOCKS_PER_DOT, blocks)
        bf16, f32 = jnp.bfloat16, jnp.float32
        dma = pltpu.SemaphoreType.DMA
        anywhere = pl.BlockSpec(memory_space=pl.ANY)
        return pl.pallas_call(
            functools.partial(kernel, (n_ep, n_node, n_pair)),
            out_shape=jax.ShapeDtypeStruct((height, width), bf16),
            in_specs=[anywhere] * 6,
            out_specs=anywhere,
            scratch_shapes=[
                pltpu.VMEM(expert_ids.T.shape, jnp.int32),
                pltpu.VMEM(gates.T.shape, f32),
                pltpu.VMEM((height, width), bf16),
                pltpu.VMEM((width, units), bf16),
                pltpu.VMEM((width, units), bf16),
                pltpu.VMEM((units, width), bf16),
                pltpu.VMEM((blocks, height, width), bf16),
                pltpu.VMEM((blocks // group, group * height, units), f32),
                pltpu.VMEM((blocks // group, group * height, units), f32),
                pltpu.VMEM((blocks // group, group * height, units), bf16),
                pltpu.VMEM((blocks, height, width), bf16),
                pltpu.VMEM((n_ep * n_node, height, width), bf16),
                pltpu.VMEM((n_node, n_ep, height, width), bf16),
                pltpu.VMEM((n_ep, height, width), bf16),
                pltpu.VMEM((n_ep, height, width), bf16),
                dma((3, steps)), dma((3,)), dma((steps,)),
                dma((steps, n_ep)), dma((steps, n_ep)),
                dma((steps, n_ep, n_node)), dma((steps, n_ep, n_node)),
                dma((steps,)), dma((steps,)),
                dma((steps,)), dma((steps,)),
                dma((steps, n_node)), dma((steps, n_node)),
                dma((steps, n_ep)), dma((steps, n_ep)),
            ],
            compiler_params=pltpu.CompilerParams(
                collective_id=0, has_side_effects=True, vmem_limit_bytes=60 * 1024 * 1024
            ),
        )(rows_in, expert_ids.T, gates.T, gate_slots, up_slots, down_slots)

    spec = P(("groups", "ep", "node", "pair"), None)
    return jax.shard_map(
        per_device,
        mesh=mesh,
        in_specs=(
            spec, spec, spec, P(),
            P("ep", None, None, ("node", "pair")),
            P("ep", None, None, ("node", "pair")),
            P("ep", None, ("node", "pair"), None),
        ),
        out_specs=spec,
        check_vma=False,
    )
```

time: 43.8 us -> 42.9 us (0.979)
  Pallas kernels: 42 us -> 41.2 us
    pallas_call x1, Pallas kernels: 42 us -> 41.2 us  [per_device(): pl.pallas_call(functools.partial(kernel, (n_ep, n_node, n_pair)), out_sha...]
where the time goes in v3:
time: 42.9 us; the launch traced here: 42.8 us
  Pallas kernels  41.2 us (96%)
  local copies, waits for them, and re-layouts  1.55 us (4%)
    pallas_call x1, Pallas kernels, per_device(): pl.pallas_call(functools.partial(kernel, (n_ep, n_node, n_pair)), out_sha...  41.2 us
    unnamed x1, local copies, waits for them, and re-layouts  1.55 us

profile of v3, /device:TPU:0, one launch (start us, length us, event | category | flops | bytes accessed | tf_op | source)
XLA Modules:
  0.0 42.8 jit_solution(670110877340457412)
XLA Ops:
  0.0 41.2 %shard_map.64 = bf16[8,7168]{1,0:T(8,128)(2,1)} custom-call(bf16[8,7168]{1,0:T(8,128)(2,1)} %rows_ref.1, s32[2,8]{1,0:T(2,128)} %bitcast.2, f32[2,8]{1,0:T(2,128)} %bitcast.3, bf16[1,2,7168,256]{3,2,1,0:T(8,128)(2,1)} %gate_hbm.1, bf16[1,2,7168,256]{3,2,1,0:T(8,128)(2,1)} %up_hbm.1, bf16[1,2,256,7168]{3,2,1,0:T(8,128)(2,1)} %down_hbm.1), custom_call_target="tpu_custom_call" | custom-call | tf_op jit(solution)/shard_map/pallas_call | solution.py:259
  41.2 1.6 %copy.8 = bf16[8,7168]{1,0:T(8,128)(2,1)} copy(bf16[8,7168]{1,0:T(8,128)(2,1)} %shard_map.64) | data formatting | bytes 229376

commit v4 on v3

--- a/solution.py
+++ b/solution.py
@@ -80,8 +80,6 @@
     peers = [dict(ep=zz) for zz in z_order[1:]] + [dict(node=xx) for xx in x_others] + [dict(pair=other)]
     for to in peers:
         pl.semaphore_signal(barrier, inc=1, device_id=to, device_id_type=pl.DeviceIdType.MESH)
-    for copy in sum(weights_in, []) + weights_out:
-        copy.start()
     ids_copy.start()
     gates_copy.start()
     pl.semaphore_wait(barrier, len(peers))
@@ -170,11 +168,14 @@
                       xs2.at[j, xx], xr2.at[j, x], node=xx))
 
     def sum_nodes(j):
+        for xx in x_others:
+            slot = node_in.at[xx, :, :, cut_out(j)]
+            remote(slot, slot, xs2.at[j, xx], xr2.at[j, xx], node=xx).wait_recv()
+        if j + ahead_back < steps_out:
+            send_nodes(j + ahead_back)
         total = part_in[pl.ds(x * n_ep, n_ep), :, cut_out(j)].astype(jnp.float32)
         total = total + part[pl.ds(c * half + x * n_ep, n_ep), :, cut_out(j)].astype(jnp.float32)
         for xx in x_others:
-            slot = node_in.at[xx, :, :, cut_out(j)]
-            remote(slot, slot, xs2.at[j, xx], xr2.at[j, xx], node=xx).wait_recv()
             total = total + node_in[xx, :, :, cut_out(j)].astype(jnp.float32)
         sums[:, :, cut_out(j)] = total.astype(jnp.bfloat16)
         for zz in z_order[1:]:
@@ -211,6 +212,8 @@
         own_out(j)
         if j == 0:
             own_nodes()
+    for copy in sum(weights_in, []) + weights_out:
+        copy.start()
     ahead_back = min(RETURN_AHEAD, steps_out)
     for t in range(steps + 2):
         if t < steps:
@@ -235,8 +238,6 @@
     for t in range(steps_out + 2):
         if t < steps_out:
             sum_nodes(t)
-        if t + ahead_back < steps_out:
-            send_nodes(t + ahead_back)
         if t >= 2:
             finish(t - 2)
     drain()

time: 42.9 us -> 43 us (level)
  no operation moved by 1% of the time
where the time goes in v4:
time: 43 us; the launch traced here: 42.8 us
  Pallas kernels  41.3 us (96%)
  local copies, waits for them, and re-layouts  1.55 us (4%)
    pallas_call x1, Pallas kernels, per_device(): pl.pallas_call(functools.partial(kernel, (n_ep, n_node, n_pair)), out_sha...  41.3 us
    unnamed x1, local copies, waits for them, and re-layouts  1.55 us

profile of v4, /device:TPU:0, one launch (start us, length us, event | category | flops | bytes accessed | tf_op | source)
XLA Modules:
  0.0 42.8 jit_solution(17374754959778054778)
XLA Ops:
  0.0 41.3 %shard_map.64 = bf16[8,7168]{1,0:T(8,128)(2,1)} custom-call(bf16[8,7168]{1,0:T(8,128)(2,1)} %rows_ref.1, s32[2,8]{1,0:T(2,128)} %bitcast.2, f32[2,8]{1,0:T(2,128)} %bitcast.3, bf16[1,2,7168,256]{3,2,1,0:T(8,128)(2,1)} %gate_hbm.1, bf16[1,2,7168,256]{3,2,1,0:T(8,128)(2,1)} %up_hbm.1, bf16[1,2,256,7168]{3,2,1,0:T(8,128)(2,1)} %down_hbm.1), custom_call_target="tpu_custom_call" | custom-call | tf_op jit(solution)/shard_map/pallas_call | solution.py:260
  41.3 1.6 %copy.8 = bf16[8,7168]{1,0:T(8,128)(2,1)} copy(bf16[8,7168]{1,0:T(8,128)(2,1)} %shard_map.64) | data formatting | bytes 229376
